TPU v7x, 32 devices: a whole 2x2x4 slice. The times are simulated.
32 devices in a mesh: dp: 32 (over z, y, x, core).
Axes of the slice: x: 2, y: 2, z: 4, core: 2. Of those that a mesh axis runs over, the one named last changes fastest.
Arguments:
- tokens: bfloat16 [2, 8192, 1024], P(None, 'dp'), may hold values from -6 to 6
- cotangent: bfloat16 [2, 8192, 1024], P(None, 'dp'), may hold values from -6 to 6
- segment_ids: int32 [2, 32, 256], P(None, 'dp'), may hold values from 0 to 3, never falling along the last dimension, each value on 1 to 128 neighbouring positions
- norm_gain: bfloat16 [1024], P('dp'), may hold values from 0.5 to 1.5
- w_query: bfloat16 [1024, 512], P('dp'), may hold values from -0.1875 to 0.1875
- w_key: bfloat16 [1024, 128], P('dp'), may hold values from -0.1875 to 0.1875
- w_value: bfloat16 [1024, 128], P('dp'), may hold values from -0.1875 to 0.1875
- w_attn_out: bfloat16 [512, 1024], P('dp'), may hold values from -1 to 1
- w_ssm_z: bfloat16 [1024, 1536], P('dp'), may hold values from -0.1875 to 0.1875
- w_ssm_x: bfloat16 [1024, 1536], P('dp'), may hold values from -0.1875 to 0.1875
- w_bc: bfloat16 [1024, 256], P('dp'), may hold values from -0.1875 to 0.1875
- w_delta: bfloat16 [1024, 24], P('dp'), may hold values from -0.1875 to 0.1875
- conv_weight: bfloat16 [1792, 4], P('dp'), may hold values from -3 to 3
- conv_bias: bfloat16 [1792], P('dp'), may hold values from -3 to 3
- ssm_gain: bfloat16 [1536], P('dp'), may hold values from 0.5 to 1.5
- w_ssm_out: bfloat16 [1536, 1024], P('dp'), may hold values from -0.15625 to 0.15625
- norm2_gain: bfloat16 [1024], P('dp'), may hold values from 0.5 to 1.5
- w_gate: bfloat16 [1024, 2048], P('dp'), may hold values from -0.1875 to 0.1875
- w_up: bfloat16 [1024, 2048], P('dp'), may hold values from -0.1875 to 0.1875
- w_down: bfloat16 [2048, 1024], P('dp'), may hold values from -0.125 to 0.125
- delta_bias: float32 [24], replicated, may hold values from -4 to -1
- decay_log: float32 [24], replicated, may hold values from -2 to 1
- skip_gain: float32 [24], replicated, may hold values from 0.5 to 1.5
Outputs:
- outputs: bfloat16 [2, 8192, 1024], P(None, 'dp')
- input_grad: float32 [2, 8192, 1024], P(None, 'dp')
- grad_norm_gain: float32 [1024], P('dp')
- grad_query: float32 [1024, 512], P('dp')
- grad_key: float32 [1024, 128], P('dp')
- grad_value: float32 [1024, 128], P('dp')
- grad_attn_out: float32 [512, 1024], P('dp')
- grad_ssm_z: float32 [1024, 1536], P('dp')
- grad_ssm_x: float32 [1024, 1536], P('dp')
- grad_bc: float32 [1024, 256], P('dp')
- grad_delta: float32 [1024, 24], P('dp')
- grad_conv_weight: float32 [1792, 4], P('dp')
- grad_conv_bias: float32 [1792], P('dp')
- grad_ssm_gain: float32 [1536], P('dp')
- grad_ssm_out: float32 [1536, 1024], P('dp')
- grad_norm2_gain: float32 [1024], P('dp')
- grad_gate: float32 [1024, 2048], P('dp')
- grad_up: float32 [1024, 2048], P('dp')
- grad_down: float32 [2048, 1024], P('dp')
- grad_delta_bias: float32 [24], replicated
- grad_decay_log: float32 [24], replicated
- grad_skip_gain: float32 [24], replicated
Inputs may be any that keep to these rules, and one draw needn't show every extreme that they name: `segment_ids`: within each row of 256 tokens of one device and micro-batch the ids never fall; each sequence has 1 to 128 tokens and one of them exactly 128.
All inputs are finite; a program needn't handle non-finite values.
Results may differ from a plain program's by a relative error of at most 0.017.
Values may be sent and summed in bfloat16 or wider, within the bound.
A program may use at most 256 MiB of HBM per device.

v0:
```python
import jax
import jax.numpy as jnp
from jax import lax
from jax.sharding import PartitionSpec as P

Q_HEADS = 8
KV_HEADS = 2
HEAD_DIM = 64
SSM_HEADS = 24
STATE = 128
KCONV = 4


EPS = 1e-05
NEG = -1e30


def matmul(left, right):
    return jnp.dot(left, right, preferred_element_type=jnp.float32)


def left_product(left, right):
    return lax.dot_general(
        left, right, (((0,), (0,)), ((), ())), preferred_element_type=jnp.float32
    )


def right_product(left, right):
    return lax.dot_general(
        left, right, (((1,), (1,)), ((), ())), preferred_element_type=jnp.float32
    )


def to_low(value):
    return value.astype(jnp.bfloat16)


def norm_forward(value, gain):
    inverse = lax.rsqrt(jnp.mean(value * value, axis=-1, keepdims=True) + EPS)
    return (value * inverse * gain, inverse)


def norm_backward(value, inverse, gain, grad):
    scaled = grad * gain
    gain_grad = jnp.sum(grad * value * inverse, axis=0)
    value_grad = inverse * scaled - value * inverse**3 * jnp.mean(
        scaled * value, axis=-1, keepdims=True
    )
    return (value_grad, gain_grad)


def silu_slope(value):
    sigma = jax.nn.sigmoid(value)
    return sigma * (1.0 + value * (1.0 - sigma))


def causal_mask(segs):
    places = jnp.arange(segs.shape[0])
    return (places[:, None] >= places[None, :]) & (segs[:, None] == segs[None, :])


def conv_masks(segs):
    masks = []
    for shift_by in range(1, KCONV):
        earlier = jnp.concatenate([jnp.full((shift_by,), -1, jnp.int32), segs[:-shift_by]])
        masks.append((segs == earlier).astype(jnp.float32)[:, None])
    return masks


def shift_down(value, shift_by):
    return jnp.concatenate(
        [jnp.zeros((shift_by, value.shape[1]), value.dtype), value[:-shift_by]], axis=0
    )


def shift_up(value, shift_by):
    return jnp.concatenate(
        [value[shift_by:], jnp.zeros((shift_by, value.shape[1]), value.dtype)], axis=0
    )


def conv_forward(conv_in, conv_weight, conv_bias, masks):
    result = conv_in * conv_weight[:, KCONV - 1]
    for shift_by in range(1, KCONV):
        result = (
            result
            + masks[shift_by - 1]
            * shift_down(conv_in, shift_by)
            * conv_weight[:, KCONV - 1 - shift_by]
        )
    return result + conv_bias


def conv_backward(grad, conv_in, conv_weight, masks):
    columns = [None] * KCONV
    columns[KCONV - 1] = jnp.sum(grad * conv_in, axis=0)
    input_grad = grad * conv_weight[:, KCONV - 1]
    for shift_by in range(1, KCONV):
        masked = grad * masks[shift_by - 1]
        columns[KCONV - 1 - shift_by] = jnp.sum(masked * shift_down(conv_in, shift_by), axis=0)
        input_grad = input_grad + shift_up(masked, shift_by) * conv_weight[:, KCONV - 1 - shift_by]
    return (input_grad, jnp.stack(columns, axis=1))


def decay(column, allowed):
    diff = column[:, None] - column[None, :]
    return jnp.where(allowed, jnp.exp(jnp.where(allowed, diff, 0.0)), 0.0)


def layer_step(inputs_low, cotangent_low, segs, params, heads, refetch):
    (
        norm_gain,
        w_query,
        w_key,
        w_value,
        w_attn_out,
        w_ssm_z,
        w_ssm_x,
        w_bc,
        w_delta,
        conv_weight,
        conv_bias,
        ssm_gain,
        w_ssm_out,
        norm2_gain,
        w_gate,
        w_up,
        w_down,
    ) = params
    delta_bias, decay_log, skip_gain = heads
    f32 = jnp.float32
    inputs = inputs_low.astype(f32)
    length = inputs.shape[0]
    group = Q_HEADS // KV_HEADS
    scale = HEAD_DIM ** (-0.5)
    width = SSM_HEADS * HEAD_DIM
    allowed = causal_mask(segs)
    masks = conv_masks(segs)
    normed, inverse1 = norm_forward(inputs, norm_gain.astype(f32))
    normed_low = to_low(normed)
    queries = to_low(matmul(normed_low, w_query)).reshape(length, KV_HEADS, group, HEAD_DIM)
    keys = to_low(matmul(normed_low, w_key)).reshape(length, KV_HEADS, HEAD_DIM)
    values = to_low(matmul(normed_low, w_value)).reshape(length, KV_HEADS, HEAD_DIM)

    def attn_probs():
        scores = jnp.einsum("igkd,jgd->gkij", queries, keys, preferred_element_type=f32) * scale
        return jnp.where(allowed, scores, NEG)

    scores = attn_probs()
    top = jnp.max(scores, axis=-1, keepdims=True)
    expo = jnp.exp(scores - top)
    total = jnp.sum(expo, axis=-1, keepdims=True)
    probs_low = to_low(expo / total)
    attended = to_low(
        jnp.einsum("gkij,jgd->igkd", probs_low, values, preferred_element_type=f32).reshape(
            length, Q_HEADS * HEAD_DIM
        )
    )
    attn_part = matmul(attended, w_attn_out)
    gate_z = matmul(normed_low, w_ssm_z)
    inner_x = matmul(normed_low, w_ssm_x)
    inner_bc = matmul(normed_low, w_bc)
    delta_raw = matmul(normed_low, w_delta)
    conv_in = jnp.concatenate([inner_x, inner_bc], axis=1)
    conv_pre = conv_forward(conv_in, conv_weight.astype(f32), conv_bias.astype(f32), masks)
    conv_out = jax.nn.silu(conv_pre)
    mixed_x = conv_out[:, :width].reshape(length, SSM_HEADS, HEAD_DIM)
    state_in = to_low(conv_out[:, width : width + STATE])
    state_out = to_low(conv_out[:, width + STATE :])
    delta = jax.nn.softplus(delta_raw + delta_bias)
    rates = -jnp.exp(decay_log)
    cumul = jnp.cumsum(delta * rates, axis=0)
    coupling = right_product(state_out, state_in)
    scaled_x = to_low(delta[:, :, None] * mixed_x).transpose(1, 0, 2)

    def head_forward(pieces):
        column, head_x = pieces
        ssd_weights = to_low(coupling * decay(column, allowed))
        return matmul(ssd_weights, head_x)

    ssd = lax.map(head_forward, (cumul.T, scaled_x))
    ssm_y = (ssd.transpose(1, 0, 2) + skip_gain[None, :, None] * mixed_x).reshape(length, width)
    gate_silu = jax.nn.silu(gate_z)
    gated = ssm_y * gate_silu
    ssm_normed, inverse3 = norm_forward(gated, ssm_gain.astype(f32))
    ssm_low = to_low(ssm_normed)
    ssm_part = matmul(ssm_low, w_ssm_out)
    resid = inputs + (attn_part + ssm_part)
    normed2, inverse2 = norm_forward(resid, norm2_gain.astype(f32))
    normed2_low = to_low(normed2)
    gate_pre = matmul(normed2_low, w_gate)
    up_pre = matmul(normed2_low, w_up)
    hidden = to_low(jax.nn.silu(gate_pre) * up_pre)
    output = resid + matmul(hidden, w_down)
    (
        back_norm,
        back_query,
        back_key,
        back_value,
        back_attn_out,
        back_ssm_z,
        back_ssm_x,
        back_bc,
        back_delta,
        back_conv,
        unused_bias,
        back_ssm_gain,
        back_ssm_out,
        back_norm2,
        back_gate,
        back_up,
        back_down,
    ) = refetch()
    upstream = cotangent_low.astype(f32)
    hidden_grad = right_product(cotangent_low, back_down)
    down_grad = left_product(hidden, cotangent_low)
    gate_sigma = jax.nn.sigmoid(gate_pre)
    gate_grad = to_low(hidden_grad * up_pre * gate_sigma * (1.0 + gate_pre * (1.0 - gate_sigma)))
    up_grad = to_low(hidden_grad * jax.nn.silu(gate_pre))
    gate_w_grad = left_product(normed2_low, gate_grad)
    up_w_grad = left_product(normed2_low, up_grad)
    normed2_grad = to_low(
        right_product(gate_grad, back_gate) + right_product(up_grad, back_up)
    ).astype(f32)
    resid_part, norm2_grad = norm_backward(resid, inverse2, back_norm2.astype(f32), normed2_grad)
    resid_grad = upstream + resid_part
    mixer_grad = to_low(resid_grad)
    attn_out_grad = left_product(attended, mixer_grad)
    ssm_out_grad = left_product(ssm_low, mixer_grad)
    attended_grad = to_low(right_product(mixer_grad, back_attn_out)).reshape(
        length, KV_HEADS, group, HEAD_DIM
    )
    ssm_normed_grad = right_product(mixer_grad, back_ssm_out)
    gated_grad, ssm_gain_grad = norm_backward(
        gated, inverse3, back_ssm_gain.astype(f32), ssm_normed_grad
    )
    ssm_y_grad = (gated_grad * gate_silu).reshape(length, SSM_HEADS, HEAD_DIM)
    gate_z_grad = to_low(gated_grad * ssm_y * silu_slope(gate_z))
    skip_grad = jnp.sum(ssm_y_grad * mixed_x, axis=(0, 2))
    mixed_grad = ssm_y_grad * skip_gain[None, :, None]
    ssd_grad = to_low(ssm_y_grad).transpose(1, 0, 2)

    def head_backward(carry, pieces):
        column, head_x, head_grad = pieces
        decays = decay(column, allowed)
        ssd_weights = to_low(coupling * decays)
        x_grad = to_low(left_product(ssd_weights, head_grad))
        weight_grad = to_low(right_product(head_grad, head_x)).astype(f32)
        spread = weight_grad * coupling * decays
        column_grad = jnp.sum(spread, axis=1) - jnp.sum(spread, axis=0)
        return (carry + weight_grad * decays, (x_grad, column_grad))

    coupling_grad, (scaled_grad, cumul_grad) = lax.scan(
        head_backward, jnp.zeros((length, length), f32), (cumul.T, scaled_x, ssd_grad)
    )
    coupling_low = to_low(coupling_grad)
    out_state_grad = to_low(matmul(coupling_low, state_in))
    in_state_grad = to_low(left_product(coupling_low, state_out))
    scaled_grad = scaled_grad.transpose(1, 0, 2).astype(f32)
    delta_grad = jnp.sum(scaled_grad * mixed_x, axis=2)
    mixed_grad = mixed_grad + scaled_grad * delta[:, :, None]
    rate_grad = jnp.cumsum(cumul_grad.T[::-1], axis=0)[::-1]
    delta_grad = delta_grad + rate_grad * rates
    decay_grad = jnp.sum(rate_grad * delta, axis=0) * rates
    delta_in_grad = delta_grad * jax.nn.sigmoid(delta_raw + delta_bias)
    bias_grad = jnp.sum(delta_in_grad, axis=0)
    delta_raw_grad = to_low(delta_in_grad)
    conv_out_grad = jnp.concatenate(
        [mixed_grad.reshape(length, width), in_state_grad.astype(f32), out_state_grad.astype(f32)],
        axis=1,
    )
    conv_pre_grad = conv_out_grad * silu_slope(conv_pre)
    conv_bias_grad = jnp.sum(conv_pre_grad, axis=0)
    conv_in_grad, conv_weight_grad = conv_backward(
        conv_pre_grad, conv_in, back_conv.astype(f32), masks
    )
    inner_x_grad = to_low(conv_in_grad[:, :width])
    inner_bc_grad = to_low(conv_in_grad[:, width:])
    probs_again = jnp.exp(attn_probs() - top) / total
    value_grad = to_low(
        jnp.einsum("gkij,igkd->jgd", to_low(probs_again), attended_grad, preferred_element_type=f32)
    ).reshape(length, KV_HEADS * HEAD_DIM)
    prob_grad = jnp.einsum("igkd,jgd->gkij", attended_grad, values, preferred_element_type=f32)
    score_grad = to_low(
        probs_again * (prob_grad - jnp.sum(prob_grad * probs_again, axis=-1, keepdims=True))
    )
    query_grad = to_low(
        jnp.einsum("gkij,jgd->igkd", score_grad, keys, preferred_element_type=f32) * scale
    ).reshape(length, Q_HEADS * HEAD_DIM)
    key_grad = to_low(
        jnp.einsum("gkij,igkd->jgd", score_grad, queries, preferred_element_type=f32) * scale
    ).reshape(length, KV_HEADS * HEAD_DIM)
    normed_grad = (
        right_product(query_grad, back_query)
        + right_product(key_grad, back_key)
        + right_product(value_grad, back_value)
        + right_product(gate_z_grad, back_ssm_z)
        + right_product(inner_x_grad, back_ssm_x)
        + right_product(inner_bc_grad, back_bc)
        + right_product(delta_raw_grad, back_delta)
    )
    normed_grad = to_low(normed_grad).astype(f32)
    input_part, norm_grad = norm_backward(inputs, inverse1, back_norm.astype(f32), normed_grad)
    input_grad = resid_grad + input_part
    grads = (
        norm_grad,
        left_product(normed_low, query_grad),
        left_product(normed_low, key_grad),
        left_product(normed_low, value_grad),
        attn_out_grad,
        left_product(normed_low, gate_z_grad),
        left_product(normed_low, inner_x_grad),
        left_product(normed_low, inner_bc_grad),
        left_product(normed_low, delta_raw_grad),
        conv_weight_grad,
        conv_bias_grad,
        ssm_gain_grad,
        ssm_out_grad,
        norm2_grad,
        gate_w_grad,
        up_w_grad,
        down_grad,
    )
    return (to_low(output), input_grad, grads, (bias_grad, decay_grad, skip_grad))


def add_tuples(first, second):
    if first is None:
        return second
    return tuple((left + right for left, right in zip(first, second)))


def per_device(
    tokens,
    cotangent,
    segment_ids,
    norm_gain,
    w_query,
    w_key,
    w_value,
    w_attn_out,
    w_ssm_z,
    w_ssm_x,
    w_bc,
    w_delta,
    conv_weight,
    conv_bias,
    ssm_gain,
    w_ssm_out,
    norm2_gain,
    w_gate,
    w_up,
    w_down,
    delta_bias,
    decay_log,
    skip_gain,
):
    heads = (delta_bias, decay_log, skip_gain)
    micro = tokens.shape[0]
    results = []
    input_grads = []
    totals = None
    head_totals = None
    for index in range(micro):
        params = (
            lax.all_gather(norm_gain, "dp", axis=0, tiled=True),
            lax.all_gather(w_query, "dp", axis=0, tiled=True),
            lax.all_gather(w_key, "dp", axis=0, tiled=True),
            lax.all_gather(w_value, "dp", axis=0, tiled=True),
            lax.all_gather(w_attn_out, "dp", axis=0, tiled=True),
            lax.all_gather(w_ssm_z, "dp", axis=0, tiled=True),
            lax.all_gather(w_ssm_x, "dp", axis=0, tiled=True),
            lax.all_gather(w_bc, "dp", axis=0, tiled=True),
            lax.all_gather(w_delta, "dp", axis=0, tiled=True),
            lax.all_gather(conv_weight, "dp", axis=0, tiled=True),
            lax.all_gather(conv_bias, "dp", axis=0, tiled=True),
            lax.all_gather(ssm_gain, "dp", axis=0, tiled=True),
            lax.all_gather(w_ssm_out, "dp", axis=0, tiled=True),
            lax.all_gather(norm2_gain, "dp", axis=0, tiled=True),
            lax.all_gather(w_gate, "dp", axis=0, tiled=True),
            lax.all_gather(w_up, "dp", axis=0, tiled=True),
            lax.all_gather(w_down, "dp", axis=0, tiled=True),
        )

        def refetch():
            return (
                lax.all_gather(norm_gain, "dp", axis=0, tiled=True),
                lax.all_gather(w_query, "dp", axis=0, tiled=True),
                lax.all_gather(w_key, "dp", axis=0, tiled=True),
                lax.all_gather(w_value, "dp", axis=0, tiled=True),
                lax.all_gather(w_attn_out, "dp", axis=0, tiled=True),
                lax.all_gather(w_ssm_z, "dp", axis=0, tiled=True),
                lax.all_gather(w_ssm_x, "dp", axis=0, tiled=True),
                lax.all_gather(w_bc, "dp", axis=0, tiled=True),
                lax.all_gather(w_delta, "dp", axis=0, tiled=True),
                lax.all_gather(conv_weight, "dp", axis=0, tiled=True),
                lax.all_gather(conv_bias, "dp", axis=0, tiled=True),
                lax.all_gather(ssm_gain, "dp", axis=0, tiled=True),
                lax.all_gather(w_ssm_out, "dp", axis=0, tiled=True),
                lax.all_gather(norm2_gain, "dp", axis=0, tiled=True),
                lax.all_gather(w_gate, "dp", axis=0, tiled=True),
                lax.all_gather(w_up, "dp", axis=0, tiled=True),
                lax.all_gather(w_down, "dp", axis=0, tiled=True),
            )

        output, input_grad, grads, head_grads = layer_step(
            tokens[index], cotangent[index], segment_ids[index, 0], params, heads, refetch
        )
        results.append(output)
        input_grads.append(input_grad)
        head_totals = add_tuples(head_totals, head_grads)
        totals = add_tuples(totals, grads)
    device_count = lax.axis_size("dp")
    packed = jnp.concatenate([member.reshape(device_count, -1) for member in totals], axis=1)
    owned_flat = lax.psum_scatter(packed, "dp", scatter_dimension=0, tiled=True)[0]
    owned = []
    offset = 0
    for member in totals:
        amount = member.size // device_count
        layout = (member.shape[0] // device_count,) + tuple(member.shape[1:])
        owned.append(owned_flat[offset : offset + amount].reshape(layout))
        offset = offset + amount
    head_sums = lax.psum((head_totals[0], head_totals[1], head_totals[2]), "dp")
    return (jnp.stack(results, axis=0), jnp.stack(input_grads, axis=0), *owned, *head_sums)


def solution(mesh):
    placed = (
        P(None, "dp", None),
        P(None, "dp", None),
        P(None, "dp", None),
        P("dp"),
        P("dp", None),
        P("dp", None),
        P("dp", None),
        P("dp", None),
        P("dp", None),
        P("dp", None),
        P("dp", None),
        P("dp", None),
        P("dp", None),
        P("dp"),
        P("dp"),
        P("dp", None),
        P("dp"),
        P("dp", None),
        P("dp", None),
        P("dp", None),
        P(),
        P(),
        P(),
    )
    return jax.shard_map(
        per_device,
        mesh=mesh,
        in_specs=placed,
        out_specs=(
            P(None, "dp", None),
            P(None, "dp", None),
            P("dp"),
            P("dp", None),
            P("dp", None),
            P("dp", None),
            P("dp", None),
            P("dp", None),
            P("dp", None),
            P("dp", None),
            P("dp", None),
            P("dp", None),
            P("dp"),
            P("dp"),
            P("dp", None),
            P("dp"),
            P("dp", None),
            P("dp", None),
            P("dp", None),
            P(),
            P(),
            P(),
        ),
        check_vma=False,
    )
```

profile of v0, /device:TPU:1, one launch (start us, length us, event | category | flops | bytes accessed | tf_op | source)
XLA Modules:
  0.0 1924.4 jit_solution(9362715492807356271)
XLA Ops:
  15.5 44.1 %all-gather = bf16[32,32,24]{1,2,0:T(8,128)(2,1)S(1)} all-gather(bf16[1,32,24]{1,2,0:T(8,128)(2,1)} %bitcast.680), channel_id=1, replica_groups=mesh['dp'=32] {'dp'}, dimensions={0}, use_global_device_ids=true | all-gather | bytes 50688 | tf_op jit(solution)/shard_map/all_gather | solution.py:374
  63.3 36.5 %all-reduce.22 = (bf16[1024]{0:T(1024)(128)(2,1)S(1)}, bf16[1792]{0:T(1024)(128)(2,1)S(1)}, bf16[1536]{0:T(1024)(128)(2,1)S(1)}, bf16[1024]{0:T(1024)(128)(2,1)S(1)}) all-reduce(bf16[1024]{0:T(1024)(128)(2,1)S(1)} %dynamic-update-slice, bf16[1792]{0:T(1024)(128)(2,1)S(1)} %dynamic-update-slice.1, ...), channel_id=1, replica_groups=mesh['dp'=32] {'dp'}, use_global_device_ids=true, to_apply=%add.16 | all-reduce | flops 5376 | bytes 21504
  102.0 42.6 %all_gather.41 = bf16[1024,256]{1,0:T(8,128)(2,1)S(1)} all-gather(bf16[32,256]{1,0:T(8,128)(2,1)S(1)} %copy-done.172), channel_id=1, replica_groups=mesh['dp'=32] {'dp'}, dimensions={0}, use_global_device_ids=true | all-gather | bytes 540672 | tf_op jit(solution)/shard_map/all_gather | solution.py:373
  145.8 37.8 %all_gather.35 = bf16[1024,128]{1,0:T(8,128)(2,1)S(1)} all-gather(bf16[32,128]{1,0:T(8,128)(2,1)S(1)} %copy-done.195), channel_id=1, replica_groups=mesh['dp'=32] {'dp'}, dimensions={0}, use_global_device_ids=true | all-gather | bytes 270336 | tf_op jit(solution)/shard_map/all_gather | solution.py:369
  185.7 38.6 %all_gather.36 = bf16[1024,128]{1,0:T(8,128)(2,1)S(1)} all-gather(bf16[32,128]{1,0:T(8,128)(2,1)S(1)} %copy-done.196), channel_id=1, replica_groups=mesh['dp'=32] {'dp'}, dimensions={0}, use_global_device_ids=true | all-gather | bytes 270336 | tf_op jit(solution)/shard_map/all_gather | solution.py:368
  228.0 37.0 %all-gather.1 = bf16[32,56,4]{1,2,0:T(4,128)(2,1)S(1)} all-gather(bf16[1,56,4]{1,2,0:T(4,128)(2,1)S(1)} %bitcast.687), channel_id=1, replica_groups=mesh['dp'=32] {'dp'}, dimensions={0}, use_global_device_ids=true | all-gather | bytes 14784 | tf_op jit(solution)/shard_map/all_gather | solution.py:375
  308.0 58.6 %while.52 = (s32[]{:T(128)}, f32[24,256,64]{1,2,0:T(8,128)}, f32[24,256]{1,0:T(8,128)}, f32[256,256]{1,0:T(8,128)S(1)}, bf16[24,256,64]{2,1,0:T(8,128)(2,1)}, /*index=5*/s32[256]{0:T(256)S(1)}, s32[]{:T(128)}) while((s32[]{:T(128)}, f32[24,256,64]{1,2,0:T(8,128)}, f32[24,256]{1,0:T(8,128)}, f32[256,256]{1,0:T(8,128)S(1)}, ...), condition=%wide.region_6.7_spmd.clone, body=%wide.region_5.6_spmd.clone.sunk | while | flops 8912898 | bytes 400473 | solution.py:181
  385.0 59.0 %while.53 = (s32[]{:T(128)}, f32[24,256,64]{1,2,0:T(8,128)}, f32[24,256]{1,0:T(8,128)}, f32[256,256]{1,0:T(8,128)S(1)}, bf16[24,256,64]{2,1,0:T(8,128)(2,1)}, /*index=5*/s32[256]{0:T(256)S(1)}, s32[]{:T(128)}) while((s32[]{:T(128)}, f32[24,256,64]{1,2,0:T(8,128)}, f32[24,256]{1,0:T(8,128)}, f32[256,256]{1,0:T(8,128)S(1)}, ...), condition=%wide.region_15.16_spmd.clone, body=%wide.region_14.15_spmd.clone.sunk | while | flops 8912898 | bytes 400473 | solution.py:181
  485.1 11.9 all-gather.25.cloned.1.call-done
  497.0 6.7 multiply_convert_fusion.10
  537.8 114.8 %while.54 = (s32[]{:T(128)}, f32[256,256]{1,0:T(8,128)}, bf16[24,256,64]{1,2,0:T(8,128)(2,1)}, f32[24,256]{1,0:T(8,128)S(1)}, bf16[24,256,64]{1,2,0:T(8,128)(2,1...) while((s32[]{:T(128)}, f32[256,256]{1,0:T(8,128)}, ...), condition=%wide.region_24.25_spmd.clone, body=%wide.region_21.24_spmd.clone.sunk | while | flops 18300676 | bytes 1756806 | solution.py:253
  656.2 6.4 multiply_reduce_fusion.8
  669.1 96.2 %while.55 = (s32[]{:T(128)}, f32[256,256]{1,0:T(8,128)S(1)}, bf16[24,256,64]{1,2,0:T(8,128)(2,1)}, f32[24,256]{1,0:T(8,128)S(1)}, bf16[24,256,64]{1,2,0:T(8,128)...) while((s32[]{:T(128)}, f32[256,256]{1,0:T(8,128)S(1)}, ...), condition=%wide.region_35.36_spmd.clone, body=%wide.region_32.35_spmd.clone.sunk | while | flops 18300676 | bytes 1756806 | solution.py:253
  889.4 6.7 convolution_add_fusion.2
  902.3 6.7 convolution_add_fusion.1
  909.0 6.6 reshape.611
  926.8 6.5 convolution_add_fusion
  939.7 7.9 convolution_add_fusion.5
  947.7 7.6 reshape.615
  955.3 8.0 convolution_add_fusion.4
  963.3 7.6 reshape.616
  976.9 7.5 reshape.617
  985.7 9.3 dynamic-update-slice.5
  1002.5 9.3 dynamic-update-slice.8
  1011.7 20.4 %dynamic-update-slice.9 = f32[32,394376]{1,0:T(8,128)} dynamic-update-slice(f32[32,394376]{1,0:T(8,128)} %dynamic-update-slice.8, f32[32,49152]{1,0:T(8,128)} %reshape.610, s32[]{} %constant.207, s32[]{} %constant.212) | dynamic-update-slice | bytes 12582916
  1032.1 20.5 %dynamic-update-slice.10 = f32[32,394376]{1,0:T(8,128)} dynamic-update-slice(f32[32,394376]{1,0:T(8,128)} %dynamic-update-slice.9, f32[32,49152]{1,0:T(8,128)} %reshape.611, s32[]{} %constant.207, s32[]{} %constant.213) | dynamic-update-slice | bytes 12582916
  1065.1 20.6 %dynamic-update-slice.16 = f32[32,394376]{1,0:T(8,128)} dynamic-update-slice(f32[32,394376]{1,0:T(8,128)} %dynamic-update-slice.15, f32[32,49152]{1,0:T(8,128)} %reshape.614, s32[]{} %constant.207, s32[]{} %constant.219) | dynamic-update-slice | bytes 12582916
  1087.3 26.0 %dynamic-update-slice.18 = f32[32,394376]{1,0:T(8,128)} dynamic-update-slice(f32[32,394376]{1,0:T(8,128)} %dynamic-update-slice.17, f32[32,65536]{1,0:T(8,128)} %reshape.615, s32[]{} %constant.207, s32[]{} %constant.221) | dynamic-update-slice | bytes 16777220
  1113.2 26.0 %dynamic-update-slice.19 = f32[32,394376]{1,0:T(8,128)} dynamic-update-slice(f32[32,394376]{1,0:T(8,128)} %dynamic-update-slice.18, f32[32,65536]{1,0:T(8,128)} %reshape.616, s32[]{} %constant.207, s32[]{} %constant.222) | dynamic-update-slice | bytes 16777220
  1139.2 25.3 %dynamic-update-slice.20 = f32[32,394376]{1,0:T(8,128)} dynamic-update-slice(f32[32,394376]{1,0:T(8,128)} %dynamic-update-slice.19, f32[32,65536]{1,0:T(8,128)} %reshape.617, s32[]{} %constant.207, s32[]{} %constant.223) | dynamic-update-slice | bytes 16777220 | tf_op jit(solution)/shard_map/concatenate | solution.py:414
  1165.7 41.0 %all-reduce.21 = (f32[24]{0:T(128)}, f32[24]{0:T(128)}, f32[24]{0:T(128)}) all-reduce(f32[24]{0:T(128)S(1)} %add.536, f32[24]{0:T(128)S(1)} %add_multiply_fusion, f32[24]{0:T(128)S(1)} %add.538), channel_id=1, replica_groups=mesh['dp'=32] {'dp'}, use_global_device_ids=true, to_apply=%region_59.60 | all-reduce | flops 72 | bytes 576 | tf_op jit(solution)/shard_map/psum | solution.py:423
  1217.7 672.7 %all-reduce.25.cloned.1.call-done = f32[32,394376]{1,0:T(8,128)} async-done(((f32[32,394376]{1,0:T(8,128)}), f32[32,394376]{1,0:T(8,128)}) %all-reduce.25.cloned.1.call-update) | async-done | bytes 50480144
  (1141 shorter events, 707.7 us)
Async XLA Ops:
  7.2 92.6 %copy-start = (bf16[2,256,1024]{2,1,0:T(8,128)(2,1)S(1)}, bf16[2,256,1024]{2,1,0:T(8,128)(2,1)}, u32[]{:S(2)}) copy-start(bf16[2,256,1024]{2,1,0:T(8,128)(2,1)} %param.31) | copy-start | bytes 3145732
  7.2 94.1 %copy-start.222 = (f32[24]{0:T(128)S(1)}, f32[24]{0:T(128)}, u32[]{:S(2)}) copy-start(f32[24]{0:T(128)} %param.51) | copy-start | bytes 292
  7.2 261.4 %all-gather.11.cloned.1.call-start = ((), (), s32[]{:S(2)}) async-start(), calls=%async_computation | async-start | bytes 1081344 | tf_op jit(solution)/shard_map/all_gather | solution.py:367
  7.9 273.1 %all-gather.15.cloned.1.call-start = ((), (), s32[]{:S(2)}) async-start(), calls=%async_computation.2 | async-start | bytes 3244032 | tf_op jit(solution)/shard_map/all_gather | solution.py:372
  8.7 447.0 %all-gather.17.cloned.1.call-start = ((), (), s32[]{:S(2)}) async-start(), calls=%async_computation.3 | async-start | bytes 3244032 | tf_op jit(solution)/shard_map/all_gather | solution.py:371
  9.4 454.6 %all-gather.19.cloned.1.call-start = ((), (), s32[]{:S(2)}) async-start(), calls=%async_computation.4 | async-start | bytes 3244032 | tf_op jit(solution)/shard_map/all_gather | solution.py:378
  10.0 458.5 %all-gather.13.cloned.1.call-start = ((), (), s32[]{:S(2)}) async-start(), calls=%async_computation.1 | async-start | bytes 1081344 | tf_op jit(solution)/shard_map/all_gather | solution.py:370
  10.6 464.8 %all-gather.21.cloned.1.call-start = ((), (), s32[]{:S(2)}) async-start(), calls=%async_computation.5 | async-start | bytes 4325376 | tf_op jit(solution)/shard_map/all_gather | solution.py:380
  11.2 469.1 %all-gather.23.cloned.1.call-start = ((), (), s32[]{:S(2)}) async-start(), calls=%async_computation.6 | async-start | bytes 4325376 | tf_op jit(solution)/shard_map/all_gather | solution.py:381
  11.9 485.1 %all-gather.25.cloned.1.call-start = ((), (), s32[]{:S(2)}) async-start(), calls=%async_computation.7 | async-start | bytes 4325376 | tf_op jit(solution)/shard_map/all_gather | solution.py:382
  12.7 1877.7 %all-reduce.25.cloned.1.call-start = ((), (), s32[]{:S(2)}) async-start(), calls=%async_computation.8 | async-start | bytes 100990976
  59.9 84.8 %copy-start.110 = (bf16[1024,24]{0,1:T(8,128)(2,1)}, bf16[1024,24]{0,1:T(8,128)(2,1)S(1)}, u32[]{:S(2)}) copy-start(bf16[1024,24]{0,1:T(8,128)(2,1)S(1)} %reshape.642) | copy-start | bytes 147460
  100.7 360.3 %copy-start.139 = (f32[256]{0:T(256)}, f32[256]{0:T(256)S(1)}, u32[]{:S(2)}) copy-start(f32[256]{0:T(256)S(1)} %get-tuple-element.707) | copy-start | bytes 3076
  101.6 124.8 %copy-start.134 = (f32[256,24]{0,1:T(8,128)}, f32[256,24]{0,1:T(8,128)S(1)}, u32[]{:S(2)}) copy-start(f32[256,24]{0,1:T(8,128)S(1)} %get-tuple-element.732) | copy-start | bytes 73732
  101.6 200.1 %copy-start.124 = (f32[256,24]{0,1:T(8,128)}, f32[256,24]{0,1:T(8,128)S(1)}, u32[]{:S(2)}) copy-start(f32[256,24]{0,1:T(8,128)S(1)} %get-tuple-element.731) | copy-start | bytes 73732
  102.0 124.4 %copy-start.136 = (f32[256,24]{0,1:T(8,128)}, f32[256,24]{0,1:T(8,128)S(1)}, u32[]{:S(2)}) copy-start(f32[256,24]{0,1:T(8,128)S(1)} %get-tuple-element.734) | copy-start | bytes 73732
  102.0 276.6 %copy-start.122 = (f32[256,24]{0,1:T(8,128)}, f32[256,24]{0,1:T(8,128)S(1)}, u32[]{:S(2)}) copy-start(f32[256,24]{0,1:T(8,128)S(1)} %get-tuple-element.733) | copy-start | bytes 73732
  145.4 147.2 %copy-start.39 = (f32[256,256]{1,0:T(8,128)}, f32[256,256]{1,0:T(8,128)S(1)}, u32[]{:S(2)}) copy-start(f32[256,256]{1,0:T(8,128)S(1)} %fusion.285) | copy-start | bytes 786436
  145.8 220.7 %copy-start.41 = (f32[256,256]{1,0:T(8,128)}, f32[256,256]{1,0:T(8,128)S(1)}, u32[]{:S(2)}) copy-start(f32[256,256]{1,0:T(8,128)S(1)} %fusion.270) | copy-start | bytes 786436
  265.2 101.3 %copy-start.114 = (f32[1792]{0:T(1024)}, f32[1792]{0:T(1024)S(1)}, u32[]{:S(2)}) copy-start(f32[1792]{0:T(1024)S(1)} %get-tuple-element.558) | copy-start | bytes 21508
  265.2 101.3 %copy-start.116 = (f32[1792]{0:T(1024)}, f32[1792]{0:T(1024)S(1)}, u32[]{:S(2)}) copy-start(f32[1792]{0:T(1024)S(1)} %get-tuple-element.559) | copy-start | bytes 21508
  265.2 101.3 %copy-start.118 = (f32[1792]{0:T(1024)}, f32[1792]{0:T(1024)S(1)}, u32[]{:S(2)}) copy-start(f32[1792]{0:T(1024)S(1)} %get-tuple-element.560) | copy-start | bytes 21508
  265.2 101.3 %copy-start.120 = (f32[1792]{0:T(1024)}, f32[1792]{0:T(1024)S(1)}, u32[]{:S(2)}) copy-start(f32[1792]{0:T(1024)S(1)} %get-tuple-element.561) | copy-start | bytes 21508
  268.4 251.7 %copy-start.112 = (f32[1024]{0:T(1024)}, f32[1024]{0:T(1024)S(1)}, u32[]{:S(2)}) copy-start(f32[1024]{0:T(1024)S(1)} %convert_element_type.383) | copy-start | bytes 12292
  268.6 98.0 %copy-start.181 = (f32[256]{0:T(256)}, f32[256]{0:T(256)S(1)}, u32[]{:S(2)}) copy-start(f32[256]{0:T(256)S(1)} %get-tuple-element.721) | copy-start | bytes 3076
  268.6 98.0 %copy-start.183 = (f32[256]{0:T(256)}, f32[256]{0:T(256)S(1)}, u32[]{:S(2)}) copy-start(f32[256]{0:T(256)S(1)} %get-tuple-element.723) | copy-start | bytes 3076
  268.6 98.0 %copy-start.185 = (f32[256]{0:T(256)}, f32[256]{0:T(256)S(1)}, u32[]{:S(2)}) copy-start(f32[256]{0:T(256)S(1)} %get-tuple-element.722) | copy-start | bytes 3076
  385.0 59.1 %copy-start.199 = (f32[24]{0:T(128)S(1)}, f32[24]{0:T(128)}, u32[]{:S(2)}) copy-start(f32[24]{0:T(128)} %param.53) | copy-start | bytes 292
  461.0 195.2 %copy-start.169 = (f32[256]{0:T(256)}, f32[256]{0:T(256)S(1)}, u32[]{:S(2)}) copy-start(f32[256]{0:T(256)S(1)} %get-tuple-element.715) | copy-start | bytes 3076
  464.0 60.9 %copy-start.163 = (f32[256]{0:T(256)}, f32[256]{0:T(256)S(1)}, u32[]{:S(2)}) copy-start(f32[256]{0:T(256)S(1)} %get-tuple-element.711) | copy-start | bytes 3076
  470.8 49.4 %copy-start.165 = (f32[256]{0:T(256)}, f32[256]{0:T(256)S(1)}, u32[]{:S(2)}) copy-start(f32[256]{0:T(256)S(1)} %get-tuple-element.713) | copy-start | bytes 3076
  470.8 49.4 %copy-start.173 = (f32[256]{0:T(256)}, f32[256]{0:T(256)S(1)}, u32[]{:S(2)}) copy-start(f32[256]{0:T(256)S(1)} %get-tuple-element.712) | copy-start | bytes 3076
  (204 other events, 1079.9 us)
Sparse Core Ops, SparseCore 0:
  10.9 56.3 all-gather.10
  70.1 58.8 all-gather.14
  131.9 58.3 all-gather.16
  193.0 57.8 all-gather.18
  253.6 52.3 all-gather.12
  308.7 61.1 all-gather.20
  372.8 60.7 all-gather.22
  436.4 60.5 all-gather.24
  1164.8 725.5 all-reduce.24
where the time goes:
time: 1950 us; the launch traced here: 1920 us
  waiting for transfers between devices  690 us (35%)
  matrix products  451 us (23%)
  local copies, waits for them, and re-layouts  411 us (21%)
  blocking collectives  278 us (14%)
  other arithmetic  76.3 us (4%)
    unnamed x10, waiting for transfers between devices  678 us
    unnamed x483, local copies, waits for them, and re-layouts  190 us
    dot_general x74, matrix products, left_product(): lax.dot_general(left, right, (((0,), (0,)), ((), ())), preferred_element_...  174 us
    dot_general x74, matrix products, matmul(): return jnp.dot(left, right, preferred_element_type=jnp.float32)  135 us
    dot_general x74, matrix products, right_product(): lax.dot_general(left, right, (((1,), (1,)), ((), ())), preferred_element_...  119 us
    dynamic_slice x96, local copies, waits for them, and re-layouts, layer_step(): ssd = lax.map(head_forward, (cumul.T, scaled_x))  67.6 us
    reshape x12, local copies, waits for them, and re-layouts, per_device(): member.reshape(device_count, -1)  53.1 us
    all_gather x1, blocking collectives, per_device(): lax.all_gather(w_delta, 'dp', axis=0, tiled=True)  44.1 us
  transfers between devices with their start and end apart: 9, of which 2 were waited for; matrix products, arithmetic and copies ran while one was open for 12% of the time, Pallas kernels for 0%

commit v1 on v0

v1 whole, which is shorter than its diff:
```python
import jax
import jax.numpy as jnp
from jax import lax
from jax.sharding import PartitionSpec as P

Q_HEADS = 8
KV_HEADS = 2
HEAD_DIM = 64
SSM_HEADS = 24
STATE = 128
KCONV = 4


EPS = 1e-05
NEG = -1e30


def matmul(left, right):
    return jnp.dot(left, right, preferred_element_type=jnp.float32)


def left_product(left, right):
    return lax.dot_general(
        left, right, (((0,), (0,)), ((), ())), preferred_element_type=jnp.float32
    )


def right_product(left, right):
    return lax.dot_general(
        left, right, (((1,), (1,)), ((), ())), preferred_element_type=jnp.float32
    )


def to_low(value):
    return value.astype(jnp.bfloat16)


def norm_forward(value, gain):
    inverse = lax.rsqrt(jnp.mean(value * value, axis=-1, keepdims=True) + EPS)
    return (value * inverse * gain, inverse)


def norm_backward(value, inverse, gain, grad):
    scaled = grad * gain
    gain_grad = jnp.sum(grad * value * inverse, axis=0)
    value_grad = inverse * scaled - value * inverse**3 * jnp.mean(
        scaled * value, axis=-1, keepdims=True
    )
    return (value_grad, gain_grad)


def silu_slope(value):
    sigma = jax.nn.sigmoid(value)
    return sigma * (1.0 + value * (1.0 - sigma))


def shift_down(value, by):
    return jnp.pad(value, ((0, 0), (by, 0), (0, 0)))[:, : value.shape[1]]


def shift_up(value, by):
    return jnp.pad(value, ((0, 0), (0, by), (0, 0)))[:, by:]


def batched(equation, left, right):
    return jnp.einsum(equation, left, right, preferred_element_type=jnp.float32)


def pack_vectors(vectors, rows):
    flat = jnp.concatenate([vector.reshape(-1) for vector in vectors])
    wide = -(-flat.size // rows)
    return jnp.pad(flat, (0, rows * wide - flat.size)).reshape(rows, wide)


def per_device(
    tokens,
    cotangent,
    segment_ids,
    norm_gain,
    w_query,
    w_key,
    w_value,
    w_attn_out,
    w_ssm_z,
    w_ssm_x,
    w_bc,
    w_delta,
    conv_weight,
    conv_bias,
    ssm_gain,
    w_ssm_out,
    norm2_gain,
    w_gate,
    w_up,
    w_down,
    delta_bias,
    decay_log,
    skip_gain,
):
    f32 = jnp.float32
    count = lax.axis_size("dp")
    micro, length, model = tokens.shape
    total = micro * length
    rows = w_query.shape[0]
    group = Q_HEADS // KV_HEADS
    scale = HEAD_DIM ** (-0.5)
    width = SSM_HEADS * HEAD_DIM
    chan = width + 2 * STATE
    q_width, kv_width = Q_HEADS * HEAD_DIM, KV_HEADS * HEAD_DIM

    vectors = (norm_gain, conv_weight, conv_bias, ssm_gain, norm2_gain)
    small = pack_vectors(vectors, rows)
    main_width = q_width + 2 * kv_width + width + chan
    tail_width = -(-(SSM_HEADS + small.shape[1]) // 128) * 128
    spare = tail_width - SSM_HEADS - small.shape[1]
    own_in = jnp.concatenate(
        [
            w_query,
            w_key,
            w_value,
            w_ssm_z,
            w_ssm_x,
            w_bc,
            w_delta,
            small,
            jnp.zeros((rows, spare), small.dtype),
        ],
        axis=1,
    )
    w_in = lax.all_gather(own_in, "dp", axis=0, tiled=True)
    own_mix = jnp.concatenate([w_attn_out, w_ssm_out], axis=0)
    w_mix = lax.all_gather(own_mix, "dp", axis=0, tiled=True)
    w_ff = lax.all_gather(jnp.concatenate([w_gate, w_up], axis=1), "dp", axis=0, tiled=True)
    w_back = lax.all_gather(w_down, "dp", axis=0, tiled=True)
    packed = w_in[:, main_width + SSM_HEADS : main_width + SSM_HEADS + small.shape[1]]
    packed = packed.reshape(count, -1)
    gains = []
    offset = 0
    for vector in vectors:
        part = packed[:, offset : offset + vector.size]
        gains.append(part.reshape((count * vector.shape[0],) + vector.shape[1:]).astype(f32))
        offset += vector.size
    gain1, taps, bias, gain3, gain2 = gains
    attn_rows = w_attn_out.shape[0]
    w_mix = w_mix.reshape(count, own_mix.shape[0], model)
    w_attn = w_mix[:, :attn_rows].reshape(-1, model)
    w_ssm = w_mix[:, attn_rows:].reshape(-1, model)
    ff = w_gate.shape[1]

    segs = segment_ids[:, 0]
    places = jnp.arange(length)
    causal = places[:, None] >= places[None, :]
    allowed = causal[None] & (segs[:, :, None] == segs[:, None, :])
    masks = []
    for by in range(1, KCONV):
        earlier = jnp.pad(segs, ((0, 0), (by, 0)), constant_values=-1)[:, :length]
        masks.append((segs == earlier).astype(f32)[:, :, None])
    inputs = tokens.reshape(total, model).astype(f32)
    normed, inverse1 = norm_forward(inputs, gain1)
    normed_low = to_low(normed)
    projected = matmul(normed_low, w_in)
    cut = q_width
    queries = to_low(projected[:, :cut]).reshape(micro, length, KV_HEADS, group, HEAD_DIM)
    keys = to_low(projected[:, cut : cut + kv_width]).reshape(micro, length, KV_HEADS, HEAD_DIM)
    cut += kv_width
    values = to_low(projected[:, cut : cut + kv_width]).reshape(micro, length, KV_HEADS, HEAD_DIM)
    cut += kv_width
    gate_z = projected[:, cut : cut + width]
    cut += width
    conv_in = projected[:, cut : cut + chan].reshape(micro, length, chan)
    delta_raw = projected[:, main_width : main_width + SSM_HEADS].reshape(micro, length, SSM_HEADS)

    scores = batched("migkd,mjgd->mgkij", queries, keys) * scale
    scores = jnp.where(allowed[:, None, None], scores, NEG)
    expo = jnp.exp(scores - jnp.max(scores, axis=-1, keepdims=True))
    probs = expo / jnp.sum(expo, axis=-1, keepdims=True)
    probs_low = to_low(probs)
    attended = to_low(batched("mgkij,mjgd->migkd", probs_low, values).reshape(total, q_width))

    conv_pre = conv_in * taps[:, KCONV - 1] + bias
    for by in range(1, KCONV):
        conv_pre += masks[by - 1] * shift_down(conv_in, by) * taps[:, KCONV - 1 - by]
    conv_out = jax.nn.silu(conv_pre)
    mixed_x = conv_out[:, :, :width].reshape(micro, length, SSM_HEADS, HEAD_DIM)
    state_in = to_low(conv_out[:, :, width : width + STATE])
    state_out = to_low(conv_out[:, :, width + STATE :])
    delta = jax.nn.softplus(delta_raw + delta_bias)
    rates = -jnp.exp(decay_log)
    lower = causal.astype(f32)
    cumul = jnp.einsum("ij,mjh->mhi", lower, delta * rates, precision=lax.Precision.HIGHEST)
    coupling = batched("mis,mjs->mij", state_out, state_in)
    scaled_x = to_low(delta[..., None] * mixed_x).transpose(0, 2, 1, 3)
    diff = cumul[:, :, :, None] - cumul[:, :, None, :]
    near = allowed[:, None]
    decays = jnp.where(near, jnp.exp(jnp.where(near, diff, 0.0)), 0.0)
    ssd_weights = to_low(coupling[:, None] * decays)
    ssd = batched("mhij,mhjd->mhid", ssd_weights, scaled_x)
    ssm_y = (ssd.transpose(0, 2, 1, 3) + skip_gain[:, None] * mixed_x).reshape(total, width)
    gate_silu = jax.nn.silu(gate_z)
    gated = ssm_y * gate_silu
    ssm_normed, inverse3 = norm_forward(gated, gain3)
    ssm_low = to_low(ssm_normed)
    resid = inputs + (matmul(attended, w_attn) + matmul(ssm_low, w_ssm))
    normed2, inverse2 = norm_forward(resid, gain2)
    normed2_low = to_low(normed2)
    pre = matmul(normed2_low, w_ff)
    gate_pre, up_pre = pre[:, :ff], pre[:, ff:]
    gate_sigma = jax.nn.sigmoid(gate_pre)
    hidden = to_low(gate_pre * gate_sigma * up_pre)
    output = to_low(resid + matmul(hidden, w_back))

    upstream = cotangent.reshape(total, model)
    grad_back = to_low(left_product(hidden, upstream))
    owned_back = lax.psum_scatter(grad_back, "dp", scatter_dimension=0, tiled=True)
    hidden_grad = right_product(upstream, w_back)
    gate_grad = to_low(hidden_grad * up_pre * gate_sigma * (1.0 + gate_pre * (1.0 - gate_sigma)))
    up_grad = to_low(hidden_grad * gate_pre * gate_sigma)
    pre_grad = jnp.concatenate([gate_grad, up_grad], axis=1)
    grad_ff = to_low(left_product(normed2_low, pre_grad))
    owned_ff = lax.psum_scatter(grad_ff, "dp", scatter_dimension=0, tiled=True)
    normed2_grad = to_low(right_product(pre_grad, w_ff)).astype(f32)
    resid_part, gain2_grad = norm_backward(resid, inverse2, gain2, normed2_grad)
    resid_grad = upstream.astype(f32) + resid_part
    mixer_grad = to_low(resid_grad)
    grad_mix = jnp.concatenate(
        [
            to_low(left_product(attended, mixer_grad)).reshape(count, -1, model),
            to_low(left_product(ssm_low, mixer_grad)).reshape(count, -1, model),
        ],
        axis=1,
    ).reshape(-1, model)
    owned_mix = lax.psum_scatter(grad_mix, "dp", scatter_dimension=0, tiled=True)

    ssm_normed_grad = right_product(mixer_grad, w_ssm)
    gated_grad, gain3_grad = norm_backward(gated, inverse3, gain3, ssm_normed_grad)
    ssm_y_grad = (gated_grad * gate_silu).reshape(micro, length, SSM_HEADS, HEAD_DIM)
    gate_z_grad = to_low(gated_grad * ssm_y * silu_slope(gate_z))
    skip_grad = jnp.sum(ssm_y_grad * mixed_x, axis=(0, 1, 3))
    ssd_grad = to_low(ssm_y_grad).transpose(0, 2, 1, 3)
    scaled_grad = to_low(batched("mhij,mhid->mhjd", ssd_weights, ssd_grad))
    weights_grad = to_low(batched("mhid,mhjd->mhij", ssd_grad, scaled_x)).astype(f32)
    damped = weights_grad * decays
    coupling_low = to_low(jnp.sum(damped, axis=1))
    spread = damped * coupling[:, None]
    cumul_grad = jnp.sum(spread, axis=3) - jnp.sum(spread, axis=2)
    out_state_grad = to_low(batched("mij,mjs->mis", coupling_low, state_in)).astype(f32)
    in_state_grad = to_low(batched("mij,mis->mjs", coupling_low, state_out)).astype(f32)
    scaled_grad = scaled_grad.transpose(0, 2, 1, 3).astype(f32)
    mixed_grad = ssm_y_grad * skip_gain[:, None] + scaled_grad * delta[..., None]
    rate_grad = jnp.einsum("ij,mhi->mjh", lower, cumul_grad, precision=lax.Precision.HIGHEST)
    delta_grad = jnp.sum(scaled_grad * mixed_x, axis=3) + rate_grad * rates
    decay_grad = jnp.sum(rate_grad * delta, axis=(0, 1)) * rates
    delta_in_grad = delta_grad * jax.nn.sigmoid(delta_raw + delta_bias)
    bias_grad = jnp.sum(delta_in_grad, axis=(0, 1))
    delta_raw_grad = to_low(delta_in_grad).reshape(total, SSM_HEADS)
    conv_out_grad = jnp.concatenate(
        [mixed_grad.reshape(micro, length, width), in_state_grad, out_state_grad], axis=2
    )
    conv_pre_grad = conv_out_grad * silu_slope(conv_pre)
    conv_bias_grad = jnp.sum(conv_pre_grad, axis=(0, 1))
    columns = [None] * KCONV
    columns[KCONV - 1] = jnp.sum(conv_pre_grad * conv_in, axis=(0, 1))
    conv_in_grad = conv_pre_grad * taps[:, KCONV - 1]
    for by in range(1, KCONV):
        masked = conv_pre_grad * masks[by - 1]
        columns[KCONV - 1 - by] = jnp.sum(masked * shift_down(conv_in, by), axis=(0, 1))
        conv_in_grad += shift_up(masked, by) * taps[:, KCONV - 1 - by]
    taps_grad = jnp.stack(columns, axis=1)

    attended_grad = to_low(right_product(mixer_grad, w_attn)).reshape(
        micro, length, KV_HEADS, group, HEAD_DIM
    )
    value_grad = to_low(batched("mgkij,migkd->mjgd", probs_low, attended_grad))
    prob_grad = batched("migkd,mjgd->mgkij", attended_grad, values)
    score_grad = to_low(probs * (prob_grad - jnp.sum(prob_grad * probs, axis=-1, keepdims=True)))
    query_grad = to_low(batched("mgkij,mjgd->migkd", score_grad, keys) * scale)
    key_grad = to_low(batched("mgkij,migkd->mjgd", score_grad, queries) * scale)

    joined = jnp.concatenate(
        [
            query_grad.reshape(total, q_width),
            key_grad.reshape(total, kv_width),
            value_grad.reshape(total, kv_width),
            gate_z_grad,
            to_low(conv_in_grad).reshape(total, chan),
            delta_raw_grad,
            jnp.zeros((total, tail_width - SSM_HEADS), jnp.bfloat16),
        ],
        axis=1,
    )
    normed_grad = to_low(right_product(joined, w_in)).astype(f32)
    input_part, gain1_grad = norm_backward(inputs, inverse1, gain1, normed_grad)
    input_grad = resid_grad + input_part
    grad_main = to_low(left_product(normed_low, joined[:, :main_width]))
    grad_delta = to_low(left_product(normed_low, delta_raw_grad))
    vector_grads = (gain1_grad, taps_grad, conv_bias_grad, gain3_grad, gain2_grad)
    flat = jnp.concatenate([to_low(grad).reshape(count, -1) for grad in vector_grads], axis=1)
    flat = jnp.pad(flat, ((0, 0), (0, small.size - flat.shape[1])))
    grad_in = jnp.concatenate(
        [
            grad_main,
            grad_delta,
            flat.reshape(model, small.shape[1]),
            jnp.zeros((model, spare), jnp.bfloat16),
        ],
        axis=1,
    )
    owned_in = lax.psum_scatter(grad_in, "dp", scatter_dimension=0, tiled=True).astype(f32)
    head_sums = lax.psum(jnp.concatenate([bias_grad, decay_grad, skip_grad]), "dp")

    bounds = [0, q_width, q_width + kv_width, q_width + 2 * kv_width]
    bounds += [bounds[-1] + width, bounds[-1] + 2 * width, main_width, main_width + SSM_HEADS]
    pieces = [owned_in[:, low:high] for low, high in zip(bounds[:-1], bounds[1:])]
    grad_query, grad_key, grad_value, grad_z, grad_x, grad_bc, grad_dt = pieces
    flat = owned_in[:, bounds[-1] : bounds[-1] + small.shape[1]].reshape(-1)
    owned = []
    offset = 0
    for vector in vectors:
        owned.append(flat[offset : offset + vector.size].reshape(vector.shape))
        offset += vector.size
    owned_mix = owned_mix.astype(f32)
    owned_ff = owned_ff.astype(f32)
    return (
        output.reshape(tokens.shape),
        input_grad.reshape(tokens.shape),
        owned[0],
        grad_query,
        grad_key,
        grad_value,
        owned_mix[:attn_rows],
        grad_z,
        grad_x,
        grad_bc,
        grad_dt,
        owned[1],
        owned[2],
        owned[3],
        owned_mix[attn_rows:],
        owned[4],
        owned_ff[:, :ff],
        owned_ff[:, ff:],
        owned_back.astype(f32),
        head_sums[:SSM_HEADS],
        head_sums[SSM_HEADS : 2 * SSM_HEADS],
        head_sums[2 * SSM_HEADS :],
    )


def solution(mesh):
    placed = (
        P(None, "dp", None),
        P(None, "dp", None),
        P(None, "dp", None),
        P("dp"),
        P("dp", None),
        P("dp", None),
        P("dp", None),
        P("dp", None),
        P("dp", None),
        P("dp", None),
        P("dp", None),
        P("dp", None),
        P("dp", None),
        P("dp"),
        P("dp"),
        P("dp", None),
        P("dp"),
        P("dp", None),
        P("dp", None),
        P("dp", None),
        P(),
        P(),
        P(),
    )
    return jax.shard_map(
        per_device,
        mesh=mesh,
        in_specs=placed,
        out_specs=(
            P(None, "dp", None),
            P(None, "dp", None),
            P("dp"),
            P("dp", None),
            P("dp", None),
            P("dp", None),
            P("dp", None),
            P("dp", None),
            P("dp", None),
            P("dp", None),
            P("dp", None),
            P("dp", None),
            P("dp"),
            P("dp"),
            P("dp", None),
            P("dp"),
            P("dp", None),
            P("dp", None),
            P("dp", None),
            P(),
            P(),
            P(),
        ),
        check_vma=False,
    )
```

time: 1950 us -> 905 us (0.46)
  matrix products: 451 us -> 143 us
  local copies, waits for them, and re-layouts: 411 us -> 128 us
  blocking collectives: 278 us -> 39 us
  waiting for transfers between devices: 690 us -> 512 us
  other arithmetic: 76.3 us -> 55 us
    unnamed x10 -> x8, waiting for transfers between devices: 678 us -> 0.64 us
    reduce_scatter x0 -> x4, waiting for transfers between devices: none -> 326 us  [the longest x1 136 us: per_device(): owned_ff = lax.psum_scatter(grad_ff, 'dp', scatter_dimension=0, tiled=True)]
    all_gather x5 -> x0, blocking collectives: 200 us -> none  [the longest x1 44.1 us: per_device(): lax.all_gather(w_delta, 'dp', axis=0, tiled=True)]
    all_gather x8 -> x4, waiting for transfers between devices: 12 us -> 185 us  [the longest x1 74.1 us: per_device(): w_in = lax.all_gather(own_in, 'dp', axis=0, tiled=True)]
    unnamed x483 -> x212, local copies, waits for them, and re-layouts: 190 us -> 18.6 us
    dot_general x74 -> x6, matrix products: 174 us -> 25.5 us  [left_product(): lax.dot_general(left, right, (((0,), (0,)), ((), ())), preferred_element_...]
    dot_general x74 -> x5, matrix products: 135 us -> 29.3 us  [matmul(): return jnp.dot(left, right, preferred_element_type=jnp.float32)]
    dot_general x74 -> x5, matrix products: 119 us -> 40.8 us  [right_product(): lax.dot_general(left, right, (((1,), (1,)), ((), ())), preferred_element_...]
  transfers between devices with their start and end apart: 9 -> 8, of which waited for: 2 -> 7; matrix products, arithmetic and copies ran while one was open for 12% -> 32% of each run, Pallas kernels for 0% -> 0%
where the time goes in v1:
time: 905 us; the launch traced here: 894 us
  waiting for transfers between devices  512 us (57%)
  matrix products  143 us (16%)
  local copies, waits for them, and re-layouts  128 us (14%)
  other arithmetic  55 us (6%)
  blocking collectives  39 us (4%)
  between operations  16 us (2%)
    reduce_scatter x1, waiting for transfers between devices, per_device(): owned_ff = lax.psum_scatter(grad_ff, 'dp', scatter_dimension=0, tiled=True)  136 us
    reduce_scatter x1, waiting for transfers between devices, per_device(): lax.psum_scatter(grad_in, 'dp', scatter_dimension=0, tiled=True).astype(f32)  136 us
    all_gather x1, waiting for transfers between devices, per_device(): w_in = lax.all_gather(own_in, 'dp', axis=0, tiled=True)  74.1 us
    reduce_scatter x1, waiting for transfers between devices, per_device(): lax.psum_scatter(grad_back, 'dp', scatter_dimension=0, tiled=True)  54.7 us
    all_gather x1, waiting for transfers between devices, per_device(): w_mix = lax.all_gather(own_mix, 'dp', axis=0, tiled=True)  54.4 us
    all_gather x1, waiting for transfers between devices, per_device(): w_back = lax.all_gather(w_down, 'dp', axis=0, tiled=True)  51.6 us
    dot_general x11, matrix products, batched(): return jnp.einsum(equation, left, right, preferred_element_type=jnp.float32)  41.3 us
    dot_general x5, matrix products, right_product(): lax.dot_general(left, right, (((1,), (1,)), ((), ())), preferred_element_...  40.8 us
  transfers between devices with their start and end apart: 8, of which 7 were waited for; matrix products, arithmetic and copies ran while one was open for 32% of the time, Pallas kernels for 0%

profile of v1, /device:TPU:1, one launch (start us, length us, event | category | flops | bytes accessed | tf_op | source)
XLA Modules:
  0.0 893.8 jit_solution(3444302828208115213)
XLA Ops:
  21.6 54.4 %all-gather.7.cloned.1.call-done = bf16[2048,1024]{1,0:T(8,128)(2,1)} async-done(((bf16[64,1024]{1,0:T(8,128)(2,1)}), bf16[2048,1024]{1,0:T(8,128)(2,1)}) %all-gather.7.cloned.1.call-update) | async-done | bytes 4194320 | tf_op jit(solution)/shard_map/all_gather | solution.py:132
  76.1 4.1 slice.245
  82.5 74.1 %all-gather.5.cloned.1.call-done = bf16[1024,4224]{1,0:T(8,128)(2,1)} async-done(((bf16[32,4224]{1,0:T(8,128)(2,1)}), bf16[1024,4224]{1,0:T(8,128)(2,1)}) %all-gather.5.cloned.1.call-update) | async-done | bytes 8650768 | tf_op jit(solution)/shard_map/all_gather | solution.py:130
  159.1 10.2 %fusion.123 = (bf16[512,4224]{1,0:T(8,128)(2,1)}, f32[512,4224]{1,0:T(8,128)S(1)}) fusion(bf16[512,1024]{1,0:T(8,128)(2,1)S(1)} %fusion.42, bf16[1024,4224]{1,0:T(8,128)(2,1)} %all-gather.5.cloned.1.call-done), kind=kOutput, calls=%fused_computation.224 | convolution fusion | flops 4431347712 | bytes 22675456 | tf_op jit(solution)/shard_map/dot_general | solution.py:19
  176.4 4.6 fusion.115
  187.4 5.9 bitcast_add_fusion
  193.3 4.3 copy.250
  197.6 4.7 reshape.361
  214.0 4.7 fusion.124
  231.3 4.9 all-gather.9.cloned.1.call-done
  236.2 11.8 %fusion.108 = f32[512,4096]{1,0:T(8,128)} fusion(bf16[1024,4096]{1,0:T(8,128)(2,1)} %all-gather.9.cloned.1.call-done, f32[512,1024]{1,0:T(8,128)} %get-tuple-element.179, f32[1024]{0:T(1024)S(1)} %reshape.351, f32[512]{0:T(512)S(1)} %get-tuple-element.167), kind=kOutput, calls=%fused_computation.212 | convolution fusion | flops 4296540160 | bytes 18880512 | tf_op jit(solution)/shard_map/dot_general | solution.py:19
  248.0 51.6 %all-gather.11.cloned.1.call-done = bf16[2048,1024]{1,0:T(8,128)(2,1)} async-done(((bf16[64,1024]{1,0:T(8,128)(2,1)}), bf16[2048,1024]{1,0:T(8,128)(2,1)}) %all-gather.11.cloned.1.call-update) | async-done | bytes 4194320 | tf_op jit(solution)/shard_map/all_gather | solution.py:134
  299.5 10.6 %multiply_convert_fusion.4 = (bf16[512,2048]{1,0:T(8,128)(2,1)S(1)}, bf16[512,2048]{1,0:T(8,128)(2,1)S(1)}, bf16[512,2048]{1,0:T(8,128)(2,1)}) fusion(f32[512,4096]{1,0:T(8,128)} %fusion.108, bf16[512,1024]{1,0:T(8,128)(2,1)} %bitcast.179, bf16[2048,1024]{1,0:T(8,128)(2,1)} %all-gather.11.cloned.1.call-done), kind=kOutput, calls=%fused_computation.21 | convolution fusion | flops 2164260864 | bytes 19922944 | tf_op jit(solution)/shard_map/dot_general | solution.py:29
  310.2 10.3 %fusion.35 = (bf16[1024]{0:T(1024)(128)(2,1)}, f32[512]{0:T(512)S(1)}, bf16[512,1024]{1,0:T(8,128)(2,1)S(1)}) fusion(f32[512,1024]{1,0:T(8,128)S(1)} %copy-done.8, f32[512]{0:T(512)S(1)} %get-tuple-element.167, f32[1024]{0:T(1024)S(1)} %reshape.351, bf16[1024,4096]{1,0:T(8,128)(2,1)} %all-gather.9.cloned.1.call-done, ...), kind=kOutput, calls=%fused_computation.83 | convolution fusion | flops 4307548672 | bytes 15738880 | tf_op jit(solution)/shard_map/dot_general | solution.py:29
  328.1 6.0 multiply_reduce_fusion.4
  334.1 5.8 fusion.19
  343.6 5.2 reshape.335
  352.2 8.7 fusion.21
  364.5 9.5 %fusion.3 = (f32[2,24,256]{2,1,0:T(8,128)}, f32[2,24,256]{2,1,0:T(8,128)}, bf16[2,256,256]{2,1,0:T(8,128)(2,1)S(1)}) fusion(f32[2,24,256]{2,1,0:T(8,128)S(1)} %copy-done.91, f32[2,256,256]{2,1,0:T(8,128)} %copy-done.29, pred[2,256,256]{2,1,0:T(8,128)(4,1)S(1)} %copy-done.37, f32[2,256,24,64]{1,3,2,0:T(8,128)} %bitcast.185, f32[2,256,24]{1,2,0:T(8,128)S(1)} %copy-done.48, ...), kind=kOutput, calls=%fused_computation.6 | convolution fusion | flops 435527680 | bytes 5832704 | tf_op jit(solution)/shard_map/mhid,mhjd->mhij/dot_general | solution.py:66
  377.1 4.4 convolution_convert_fusion.2
  382.2 9.0 %multiply_reduce_fusion.3 = (bf16[1792]{0:T(1024)(128)(2,1)S(1)}, bf16[1792]{0:T(1024)(128)(2,1)S(1)}, bf16[1792]{0:T(1024)(128)(2,1)S(1)}, f32[2,256,1792]{2,1,...) fusion(f32[2,256,1792]{2,1,0:T(8,128)} %bitcast.170, ...), kind=kLoop, calls=%fused_computation.44 | loop fusion | flops 17427200 | bytes 25707008 | tf_op jit(solution)/shard_map/reduce_sum | solution.py:266
  391.2 5.4 fusion.111
  431.5 5.7 constant_dynamic-update-slice_fusion.1
  439.3 7.9 concatenate.42
  447.3 10.8 %fusion.37 = (bf16[1024]{0:T(1024)(128)(2,1)S(1)}, f32[512]{0:T(512)S(1)}, bf16[512,1024]{1,0:T(8,128)(2,1)}) fusion(bf16[2,256,1024]{2,1,0:T(8,128)(2,1)S(1)} %copy-done.12, f32[512]{0:T(512)S(1)} %bitcast.202, f32[1024]{0:T(1024)S(1)} %copy-done.50, bf16[512,4224]{1,0:T(8,128)(2,1)} %concatenate.42, bf16[1024,4224]{1,0:T(8,128)(2,1)} %all-gather.5.cloned.1.call-done), kind=kOutput, calls=%fused_computation.85 | convolution fusion | flops 4433902080 | bytes 15083520 | tf_op jit(solution)/shard_map/dot_general | solution.py:29
  461.5 8.9 convolution_convert_fusion.1
  470.4 13.7 %concatenate.45 = bf16[1024,4224]{1,0:T(8,128)(2,1)} concatenate(bf16[1024,4096]{1,0:T(8,128)(2,1)} %convolution_convert_fusion.1, bf16[1024,24]{1,0:T(8,128)(2,1)S(1)} %copy.222, bf16[1024,13]{1,0:T(8,128)(2,1)S(1)} %reshape.340, bf16[1024,91]{1,0:T(8,128)(2,1)S(1)} %broadcast_in_dim.40), dimensions={1} | concatenate | bytes 17301504 | tf_op jit(solution)/shard_map/concatenate | solution.py:299
  485.7 9.1 %convolution_convert_fusion = bf16[1024,4096]{1,0:T(8,128)(2,1)} fusion(bf16[512,2048]{1,0:T(8,128)(2,1)} %copy-done.100, bf16[512,2048]{1,0:T(8,128)(2,1)} %copy-done.99, f32[512,1024]{1,0:T(8,128)S(1)} %copy-done.9, f32[1024]{0:T(1024)S(1)} %copy-done.52, f32[512]{0:T(512)S(1)} %copy-done.67), kind=kOutput, calls=%fused_computation.8 | convolution fusion | flops 4309123072 | bytes 14686208 | tf_op jit(solution)/shard_map/dot_general | solution.py:23
  495.9 39.0 %psum.7 = f32[72]{0:T(128)S(1)} all-reduce(f32[72]{0:T(128)S(1)} %pad_maximum_fusion.9), channel_id=1, replica_groups=mesh['dp'=32] {'dp'}, use_global_device_ids=true, to_apply=%region_29.30 | all-reduce | flops 72 | bytes 576 | tf_op jit(solution)/shard_map/psum | solution.py:309
  546.4 54.7 %reduce-scatter.11.cloned.1.call-done = bf16[64,1024]{1,0:T(8,128)(2,1)} async-done(((bf16[2048,1024]{1,0:T(8,128)(2,1)}), bf16[64,1024]{1,0:T(8,128)(2,1)}) %reduce-scatter.11.cloned.1.call-update) | async-done | bytes 131088 | tf_op jit(solution)/shard_map/reduce_scatter | solution.py:214
  602.7 135.6 %reduce-scatter.5.cloned.1.call-done = bf16[32,4224]{1,0:T(8,128)(2,1)} async-done(((bf16[1024,4224]{1,0:T(8,128)(2,1)}), bf16[32,4224]{1,0:T(8,128)(2,1)}) %reduce-scatter.5.cloned.1.call-update) | async-done | bytes 270352 | tf_op jit(solution)/shard_map/reduce_scatter | solution.py:308
  748.8 135.9 %reduce-scatter.9.cloned.1.call-done = bf16[32,4096]{1,0:T(8,128)(2,1)} async-done(((bf16[1024,4096]{1,0:T(8,128)(2,1)}), bf16[32,4096]{1,0:T(8,128)(2,1)}) %reduce-scatter.9.cloned.1.call-update) | async-done | bytes 262160 | tf_op jit(solution)/shard_map/reduce_scatter | solution.py:220
  (353 shorter events, 146.4 us)
Async XLA Ops:
  7.2 12.6 %copy-start.81 = (s32[2,1,256]{2,1,0:T(1,128)S(1)}, s32[2,1,256]{2,1,0:T(1,128)}, u32[]{:S(2)}) copy-start(s32[2,1,256]{2,1,0:T(1,128)} %param.25) | copy-start | bytes 6148
  7.2 12.7 %copy-start.88 = (f32[24]{0:T(128)S(1)}, f32[24]{0:T(128)}, u32[]{:S(2)}) copy-start(f32[24]{0:T(128)} %param.44) | copy-start | bytes 292
  7.2 68.8 %all-gather.7.cloned.1.call-start = ((), (), s32[]{:S(2)}) async-start(), calls=%async_computation.5 | async-start | bytes 4325376 | tf_op jit(solution)/shard_map/all_gather | solution.py:132
  8.8 147.7 %all-gather.5.cloned.1.call-start = ((), (), s32[]{:S(2)}) async-start(), calls=%async_computation.4 | async-start | bytes 8921088 | tf_op jit(solution)/shard_map/all_gather | solution.py:130
  15.3 220.9 %all-gather.9.cloned.1.call-start = ((), (), s32[]{:S(2)}) async-start(), calls=%async_computation.6 | async-start | bytes 8650752 | tf_op jit(solution)/shard_map/all_gather | solution.py:133
  17.0 282.5 %all-gather.11.cloned.1.call-start = ((), (), s32[]{:S(2)}) async-start(), calls=%async_computation.7 | async-start | bytes 4325376 | tf_op jit(solution)/shard_map/all_gather | solution.py:134
  17.6 525.8 %reduce-scatter.7.cloned.1.call-start = ((), (), s32[]{:S(2)}) async-start(), calls=%async_computation.9 | async-start | bytes 4325376 | tf_op jit(solution)/shard_map/reduce_scatter | solution.py:232
  19.8 139.0 %copy-start.54 = (f32[1,2,2,128]{3,1,2,0:T(2,128)}, f32[1,2,2,128]{3,1,2,0:T(2,128)S(1)}, u32[]{:S(2)}) copy-start(f32[1,2,2,128]{3,1,2,0:T(2,128)S(1)} %copy.262) | copy-start | bytes 6148
  19.9 156.2 %copy-start.58 = (f32[2,256]{1,0:T(2,128)}, f32[2,256]{1,0:T(2,128)S(1)}, u32[]{:S(2)}) copy-start(f32[2,256]{1,0:T(2,128)S(1)} %get-tuple-element.168) | copy-start | bytes 6148
  19.9 156.2 %copy-start.60 = (f32[2,256]{1,0:T(2,128)}, f32[2,256]{1,0:T(2,128)S(1)}, u32[]{:S(2)}) copy-start(f32[2,256]{1,0:T(2,128)S(1)} %get-tuple-element.169) | copy-start | bytes 6148
  19.9 156.2 %copy-start.62 = (f32[2,256]{1,0:T(2,128)}, f32[2,256]{1,0:T(2,128)S(1)}, u32[]{:S(2)}) copy-start(f32[2,256]{1,0:T(2,128)S(1)} %get-tuple-element.170) | copy-start | bytes 6148
  76.1 82.7 %copy-start.10 = (bf16[2,256,1024]{2,1,0:T(8,128)(2,1)S(1)}, bf16[2,256,1024]{2,1,0:T(8,128)(2,1)}, u32[]{:S(2)}) copy-start(bf16[2,256,1024]{2,1,0:T(8,128)(2,1)} %param.23) | copy-start | bytes 3145732
  158.0 16.2 %copy-start.32 = (bf16[32,416]{1,0:T(8,128)(2,1)}, bf16[32,416]{1,0:T(8,128)(2,1)S(1)}, u32[]{:S(2)}) copy-start(bf16[32,416]{1,0:T(8,128)(2,1)S(1)} %reshape.318) | copy-start | bytes 79876
  223.0 97.5 %copy-start.51 = (f32[1024]{0:T(1024)}, f32[1024]{0:T(1024)S(1)}, u32[]{:S(2)}) copy-start(f32[1024]{0:T(1024)S(1)} %reshape.351) | copy-start | bytes 12292
  226.3 107.8 %copy-start.70 = (f32[512]{0:T(512)}, f32[512]{0:T(512)S(1)}, u32[]{:S(2)}) copy-start(f32[512]{0:T(512)S(1)} %get-tuple-element.164) | copy-start | bytes 6148
  226.3 107.8 %copy-start.72 = (f32[512]{0:T(512)}, f32[512]{0:T(512)S(1)}, u32[]{:S(2)}) copy-start(f32[512]{0:T(512)S(1)} %get-tuple-element.165) | copy-start | bytes 6148
  231.3 89.2 %copy-start.64 = (f32[512]{0:T(512)}, f32[512]{0:T(512)S(1)}, u32[]{:S(2)}) copy-start(f32[512]{0:T(512)S(1)} %get-tuple-element.166) | copy-start | bytes 6148
  231.3 89.2 %copy-start.66 = (f32[512]{0:T(512)}, f32[512]{0:T(512)S(1)}, u32[]{:S(2)}) copy-start(f32[512]{0:T(512)S(1)} %get-tuple-element.167) | copy-start | bytes 6148
  299.5 10.7 %copy-start.8 = (f32[512,1024]{1,0:T(8,128)S(1)}, f32[512,1024]{1,0:T(8,128)}, u32[]{:S(2)}) copy-start(f32[512,1024]{1,0:T(8,128)} %get-tuple-element.179) | copy-start | bytes 6291460
  328.0 273.0 %reduce-scatter.11.cloned.1.call-start = ((), (), s32[]{:S(2)}) async-start(), calls=%async_computation.11 | async-start | bytes 4325376 | tf_op jit(solution)/shard_map/reduce_scatter | solution.py:214
  364.5 12.6 %copy-start.19 = (bf16[2,256,1024]{2,1,0:T(8,128)(2,1)S(1)}, bf16[2,256,1024]{2,1,0:T(8,128)(2,1)}, u32[]{:S(2)}) copy-start(bf16[2,256,1024]{2,1,0:T(8,128)(2,1)} %param.24) | copy-start | bytes 3145732
  364.5 12.6 %copy-start.97 = (bf16[512,2048]{1,0:T(8,128)(2,1)S(1)}, bf16[512,2048]{1,0:T(8,128)(2,1)}, u32[]{:S(2)}) copy-start(bf16[512,2048]{1,0:T(8,128)(2,1)} %get-tuple-element.145) | copy-start | bytes 6291460
  381.5 356.8 %reduce-scatter.5.cloned.1.call-start = ((), (), s32[]{:S(2)}) async-start(), calls=%async_computation.8 | async-start | bytes 8921088 | tf_op jit(solution)/shard_map/reduce_scatter | solution.py:308
  447.2 10.9 %copy-start.77 = (bf16[1792]{0:T(1024)(128)(2,1)S(1)}, bf16[1792]{0:T(1024)(128)(2,1)}, u32[]{:S(2)}) copy-start(bf16[1792]{0:T(1024)(128)(2,1)} %get-tuple-element.115) | copy-start | bytes 10756
  447.2 11.0 %copy-start.78 = (bf16[1536]{0:T(1024)(128)(2,1)S(1)}, bf16[1536]{0:T(1024)(128)(2,1)}, u32[]{:S(2)}) copy-start(bf16[1536]{0:T(1024)(128)(2,1)} %get-tuple-element.113) | copy-start | bytes 9220
  447.3 11.1 %copy-start.80 = (bf16[1024]{0:T(1024)(128)(2,1)S(1)}, bf16[1024]{0:T(1024)(128)(2,1)}, u32[]{:S(2)}) copy-start(bf16[1024]{0:T(1024)(128)(2,1)} %get-tuple-element.120) | copy-start | bytes 6148
  447.3 11.2 %copy-start.46 = (bf16[32,224]{1,0:T(8,128)(2,1)S(1)}, bf16[32,224]{1,0:T(8,128)(2,1)}, u32[]{:S(2)}) copy-start(bf16[32,224]{1,0:T(8,128)(2,1)} %convert_element_type.345) | copy-start | bytes 43012
  447.3 11.9 %copy-start.57 = (bf16[2,256,24]{1,2,0:T(8,128)(2,1)S(1)}, bf16[2,256,24]{1,2,0:T(8,128)(2,1)}, u32[]{:S(2)}) copy-start(bf16[2,256,24]{1,2,0:T(8,128)(2,1)} %copy-done.56) | copy-start | bytes 73732
  447.3 11.9 %copy-start.79 = (f32[2,256]{1,0:T(2,128)S(1)}, f32[2,256]{1,0:T(2,128)}, u32[]{:S(2)}) copy-start(f32[2,256]{1,0:T(2,128)} %get-tuple-element.162) | copy-start | bytes 6148
  484.2 400.5 %reduce-scatter.9.cloned.1.call-start = ((), (), s32[]{:S(2)}) async-start(), calls=%async_computation.10 | async-start | bytes 8650752 | tf_op jit(solution)/shard_map/reduce_scatter | solution.py:220
  494.9 40.6 %copy-start.65 = (f32[512]{0:T(512)S(1)}, f32[512]{0:T(512)}, u32[]{:S(2)}) copy-start(f32[512]{0:T(512)} %copy-done.64) | copy-start | bytes 6148
  494.9 40.6 %copy-start.69 = (f32[512]{0:T(512)S(1)}, f32[512]{0:T(512)}, u32[]{:S(2)}) copy-start(f32[512]{0:T(512)} %copy-done.68) | copy-start | bytes 6148
  (77 other events, 376.0 us)
Sparse Core Ops, SparseCore 0:
  11.5 64.5 all-gather.6
  79.5 76.9 all-gather.4
  160.0 76.0 all-gather.8
  238.9 60.6 all-gather.10
  328.1 133.6 reduce-scatter.6
  463.9 137.0 reduce-scatter.10
  607.0 131.2 reduce-scatter.4
  740.6 144.0 reduce-scatter.8
